TPU v7x, 256 devices: a whole 4x4x8 slice. The times are simulated.
256 devices in a mesh: dp: 4 (over z_hi, core), fsdp: 64 (over x, y, z_lo).
Axes of the slice: x: 4, y: 4, z: 8 (z_hi: 2, z_lo: 4; z = z_hi * 4 + z_lo), core: 2. Of those that a mesh axis runs over, the one named last changes fastest.
Arguments:
- inputs: bfloat16 [65536, 8192], P(('dp', 'fsdp')), may hold values from -6 to 6
- cotangent: bfloat16 [65536, 512], P(('dp', 'fsdp')), may hold values from -6 to 6
- old_weight: float32 [512, 8192], P('fsdp'), may hold values from -0.0625 to 0.0625
- old_first: float32 [512, 8192], P('fsdp'), may hold values from -6 to 6
- old_second: float32 [512, 8192], P('fsdp'), may hold values from 0.1 to 2
- holder: int32 [64], replicated, may hold values from 0 to 63, each once
Outputs:
- values: bfloat16 [65536, 512], P(('dp', 'fsdp'))
- grad_input: bfloat16 [65536, 8192], P(('dp', 'fsdp'))
- new_weight: float32 [8192, 512], P('fsdp')
- new_first: float32 [8192, 512], P('fsdp')
- new_second: float32 [8192, 512], P('fsdp')
Inputs may be any that keep to these rules, and one draw needn't show every extreme that they name: `holder`: each fsdp position holds a different checkpoint block: every value of 0 to 64 - 1 appears once.
All inputs are finite; a program needn't handle non-finite values.
Results may differ from a plain program's by a relative error of at most 0.0049.
Values may be sent and summed in bfloat16 or wider, within the bound.
A program may use at most 128 MiB of HBM per device.

v0:
```python
import math

import jax
import jax.numpy as jnp
from jax import lax
from jax.sharding import PartitionSpec as P

ADAM_STEP = 20


beta_one = 0.9
beta_two = 0.95
epsilon = 1e-08
decay_rate = 0.1
learn_rate = 0.001


def adamw(gradient, weight, first_moment, second_moment):
    first_new = beta_one * first_moment + (1.0 - beta_one) * gradient
    second_new = beta_two * second_moment + (1.0 - beta_two) * gradient * gradient
    corrected = (
        first_new
        / (1.0 - beta_one**ADAM_STEP)
        / (jnp.sqrt(second_new / (1.0 - beta_two**ADAM_STEP)) + epsilon)
    )
    weight_new = weight - learn_rate * (corrected + decay_rate * weight)
    return (weight_new, first_new, second_new)


def reorder_blocks(stacked, block_order, shards):
    rows, columns = stacked.shape
    return stacked.reshape(shards, rows // shards, columns)[block_order].reshape(rows, columns)


def on_device(inputs, cotangent, old_weight, old_first, old_second, holder):
    shards = lax.axis_size("fsdp")
    replicas = lax.axis_size("dp")
    block_order = jnp.argsort(holder)
    arrived = (
        lax.all_to_all(old_weight, "fsdp", split_axis=1, concat_axis=0, tiled=True),
        lax.all_to_all(old_first, "fsdp", split_axis=1, concat_axis=0, tiled=True),
        lax.all_to_all(old_second, "fsdp", split_axis=1, concat_axis=0, tiled=True),
    )
    weight = reorder_blocks(arrived[0], block_order, shards).T
    first_moment = reorder_blocks(arrived[1], block_order, shards).T
    second_moment = reorder_blocks(arrived[2], block_order, shards).T
    gathered = lax.all_gather(weight.astype(jnp.bfloat16), "fsdp", axis=0, tiled=True)
    values = jnp.dot(inputs, gathered, preferred_element_type=jnp.float32)
    grad_input = lax.dot_general(
        cotangent, gathered, (((1,), (1,)), ((), ())), preferred_element_type=jnp.float32
    )
    values = values.astype(jnp.bfloat16)
    grad_input = grad_input.astype(jnp.bfloat16)
    total_tokens = inputs.shape[0] * replicas * shards
    loss_scale = 1.0 / math.sqrt(total_tokens)
    partial_sum = lax.psum_scatter(
        lax.dot_general(
            inputs, cotangent, (((0,), (0,)), ((), ())), preferred_element_type=jnp.float32
        )
        * loss_scale,
        "fsdp",
        scatter_dimension=0,
        tiled=True,
    )
    gradient = lax.psum(partial_sum.astype(jnp.bfloat16), "dp").astype(jnp.float32)
    new_weight, new_first, new_second = adamw(gradient, weight, first_moment, second_moment)
    return (values, grad_input, new_weight, new_first, new_second)


def solution(mesh):
    in_specs = (
        P(("dp", "fsdp"), None),
        P(("dp", "fsdp"), None),
        P("fsdp", None),
        P("fsdp", None),
        P("fsdp", None),
        P(),
    )
    out_specs = (
        P(("dp", "fsdp"), None),
        P(("dp", "fsdp"), None),
        P("fsdp", None),
        P("fsdp", None),
        P("fsdp", None),
    )
    return jax.shard_map(
        on_device, mesh=mesh, in_specs=in_specs, out_specs=out_specs, check_vma=False
    )
```

profile of v0, /device:TPU:1, one launch (start us, length us, event | category | flops | bytes accessed | tf_op | source)
XLA Modules:
  0.0 902.5 jit_solution(4941020609038303462)
XLA Ops:
  7.2 0.0 copy-start
  7.2 12.7 %all-to-all-start = ((f32[8,64,128]{2,0,1:T(8,128)}), f32[8,64,128]{2,0,1:T(8,128)S(1)}, u32[]{:S(2)}, u32[]{:S(2)}) async-start(f32[8,64,128]{2,0,1:T(8,128)} %bitcast.41), calls=%async_computation | async-start | bytes 524288 | tf_op jit(solution)/shard_map/all_to_all | solution.py:40
  19.9 0.0 all-gather.2.cloned.1.call-start
  19.9 2.7 sort.17
  22.6 8.2 all-to-all-done
  30.9 0.6 gather_fusion
  31.5 0.1 copy.13
  31.6 0.7 bitcast_convert_fusion
  32.3 0.0 all-gather.2.cloned.1.call-update
  32.3 0.0 reduce-scatter.2.cloned.1.call-start
  32.4 0.0 copy-done
  32.4 10.3 %convolution_multiply_fusion = f32[8192,512]{1,0:T(8,128)} fusion(bf16[256,8192]{1,0:T(8,128)(2,1)} %param.6, bf16[256,512]{1,0:T(8,128)(2,1)S(1)} %copy-done), kind=kOutput, calls=%fused_computation.3 | convolution fusion | flops 2151677952 | bytes 21233664 | tf_op jit(solution)/shard_map/dot_general | solution.py:57
  42.7 0.0 copy-start.1
  42.7 0.0 reduce-scatter.2.cloned.1.call-update
  42.7 0.9 copy-done.1
  43.6 21.0 %all_to_all.48 = f32[8,64,128]{2,0,1:T(8,128)S(1)} all-to-all(f32[8,64,128]{2,0,1:T(8,128)S(1)} %bitcast.42), channel_id=1, replica_groups=mesh['dp'=4,'fsdp'=64] {'fsdp'}, dimensions={1} | all-to-all | bytes 524288 | tf_op jit(solution)/shard_map/all_to_all | solution.py:41
  64.7 7.5 all-to-all-start.2
  72.2 0.0 all-reduce.2.cloned.1.call-start
  72.3 0.6 gather_fusion.1
  72.9 0.1 copy.14
  73.1 17.1 %all-to-all-done.2 = f32[8,64,128]{2,0,1:T(8,128)S(1)} async-done(((f32[8,64,128]{2,0,1:T(8,128)}), f32[8,64,128]{2,0,1:T(8,128)S(1)}, u32[]{:S(2)}, u32[]{:S(2)}) %all-to-all-start.2) | async-done | bytes 262176 | tf_op jit(solution)/shard_map/all_to_all | solution.py:42
  90.1 0.6 gather_fusion.2
  90.8 0.1 copy.15
  90.9 279.9 %all-gather.2.cloned.1.call-done = bf16[8192,512]{1,0:T(8,128)(2,1)} async-done(((bf16[128,512]{1,0:T(8,128)(2,1)}), bf16[8192,512]{1,0:T(8,128)(2,1)}) %all-gather.2.cloned.1.call-update) | async-done | bytes 8388624 | tf_op jit(solution)/shard_map/all_gather | solution.py:47
  370.9 7.7 fusion
  378.6 418.6 %reduce-scatter.2.cloned.1.call-done = f32[128,512]{1,0:T(8,128)} async-done(((f32[8192,512]{1,0:T(8,128)}), f32[128,512]{1,0:T(8,128)}) %reduce-scatter.2.cloned.1.call-update) | async-done | bytes 262160 | tf_op jit(solution)/shard_map/reduce_scatter | solution.py:56
  797.2 1.6 convert_element_type.26
  798.8 0.0 all-reduce.2.cloned.1.call-update
  798.8 6.9 fusion.1
  805.8 6.3 copy.17
  812.1 0.8 copy.16
  812.9 81.1 %all-reduce.2.cloned.1.call-done = bf16[128,512]{1,0:T(8,128)(2,1)} async-done(((bf16[128,512]{1,0:T(8,128)(2,1)}), bf16[128,512]{1,0:T(8,128)(2,1)}) %all-reduce.2.cloned.1.call-update) | async-done | bytes 131088 | tf_op jit(solution)/shard_map/psum | solution.py:65
  894.0 1.9 bitcast_subtract_fusion
  (5 shorter events, 0.1 us)
Async XLA Ops:
  7.2 25.2 %copy-start = (bf16[256,512]{1,0:T(8,128)(2,1)S(1)}, bf16[256,512]{1,0:T(8,128)(2,1)}, u32[]{:S(2)}) copy-start(bf16[256,512]{1,0:T(8,128)(2,1)} %param.7) | copy-start | bytes 786436
  7.2 23.7 %all-to-all-start = ((f32[8,64,128]{2,0,1:T(8,128)}), f32[8,64,128]{2,0,1:T(8,128)S(1)}, u32[]{:S(2)}, u32[]{:S(2)}) async-start(f32[8,64,128]{2,0,1:T(8,128)} %bitcast.41), calls=%async_computation | async-start | bytes 524288 | tf_op jit(solution)/shard_map/all_to_all | solution.py:40
  19.9 351.0 %all-gather.2.cloned.1.call-start = ((), (), s32[]{:S(2)}) async-start(), calls=%async_computation.4 | async-start | bytes 8519680 | tf_op jit(solution)/shard_map/all_gather | solution.py:47
  32.3 764.9 %reduce-scatter.2.cloned.1.call-start = ((), (), s32[]{:S(2)}) async-start(), calls=%async_computation.5 | async-start | bytes 17039360 | tf_op jit(solution)/shard_map/reduce_scatter | solution.py:56
  42.7 0.9 copy-start.1
  64.7 25.5 %all-to-all-start.2 = ((f32[8,64,128]{2,0,1:T(8,128)}), f32[8,64,128]{2,0,1:T(8,128)S(1)}, u32[]{:S(2)}, u32[]{:S(2)}) async-start(f32[8,64,128]{2,0,1:T(8,128)} %bitcast.10), calls=%async_computation.3 | async-start | bytes 524288 | tf_op jit(solution)/shard_map/all_to_all | solution.py:42
  72.2 821.8 %all-reduce.2.cloned.1.call-start = ((), (), s32[]{:S(2)}) async-start(), calls=%async_computation.6 | async-start | bytes 262144 | tf_op jit(solution)/shard_map/psum | solution.py:65
Sparse Core Ops, SparseCore 0:
  32.4 338.3 all-gather.1
  373.4 423.7 reduce-scatter.1
  800.4 93.6 all-reduce.1
where the time goes:
time: 903 us; the launch traced here: 902 us
  waiting for transfers between devices  805 us (89%)
  matrix products  25 us (3%)
  blocking collectives  21 us (2%)
  starting transfers between devices  20.4 us (2%)
  between operations  13.9 us (2%)
  local copies, waits for them, and re-layouts  10.4 us (1%)
    reduce_scatter x1, waiting for transfers between devices, on_device(): lax.psum_scatter(lax.dot_general(inputs, cotangent, (((0,), (0,)), ((), (...  419 us
    all_gather x1, waiting for transfers between devices, on_device(): lax.all_gather(weight.astype(jnp.bfloat16), 'fsdp', axis=0, tiled=True)  280 us
    psum x1, waiting for transfers between devices, on_device(): lax.psum(partial_sum.astype(jnp.bfloat16), 'dp').astype(jnp.float32)  81.1 us
    all_to_all x1, blocking collectives, on_device(): lax.all_to_all(old_first, 'fsdp', split_axis=1, concat_axis=0, tiled=True)  21 us
  transfers between devices with their start and end apart: 5, of which 5 were waited for; matrix products, arithmetic and copies ran while one was open for 4% of the time, Pallas kernels for 0%

commit v1 on v0

v1 whole, which is shorter than its diff:
```python
import functools

import jax
import jax.numpy as jnp
from jax import lax
from jax.experimental import pallas as pl
from jax.experimental.pallas import tpu as pltpu
from jax.sharding import PartitionSpec as P

ADAM_STEP = 20
beta_one = 0.9
beta_two = 0.95
epsilon = 1e-08
decay_rate = 0.1
learn_rate = 0.001

MESH = pl.DeviceIdType.MESH
TOK, D, KV = 256, 8192, 512
HALF = KV // 2
PARTS = ((0, 96), (96, 96), (192, 64))
RS_ORDER = ((0, 1, 2), (1, 2, 0), (2, 0, 1))
AG_ORDER = ((2, 1, 0), (0, 2, 1), (1, 0, 2))
MOVE_ORDER = ((0, 1, 2), (1, 2, 0), (2, 0, 1))
XCHUNKS = 4


def device(x, y, z, core):
    return ((z // 4) * 2 + core, x * 16 + y * 4 + lax.rem(z, 4))


def coordinates():
    dp = lax.axis_index("dp")
    f = lax.axis_index("fsdp")
    core = lax.rem(dp, 2)
    return f // 16, lax.rem(f // 4, 4), (dp // 2) * 4 + lax.rem(f, 4), core


def kernel(
    x_hbm, cot_ref, w_ref, f_ref, s_ref, inv_ref,
    val_ref, gin_ref, nw_ref, nf_ref, ns_ref,
    x_own, x_sib, cot_sib, cot_t, grad, gath, wcol, acc,
    rl0, rr0, ha0, hb0, rl1, rr1, ha1, hb1, rl2, rr2, ha2, hb2,
    mid_a, mid_b, mid_c, zsend, zrecv, gfull,
    loc_sem, xs_sem, xr_sem, ag_s, ag_r, sh_s, sh_r, rs_s, rs_r, mv_s, mv_r, fin_s, fin_r,
):
    x, y, z, core = coordinates()
    me = (x, y, lax.rem(z, 4))
    size = (4, 4, 8)
    real = (x, y, z)
    olds = (w_ref, f_ref, s_ref)
    mids = (mid_a, mid_b, mid_c)
    recv = ((rl0, rr0, ha0, hb0), (rl1, rr1, ha1, hb1), (rl2, rr2, ha2, hb2))

    def peer(axis, step):
        at = list(real)
        at[axis] = lax.rem(at[axis] + step + size[axis], size[axis])
        return device(*at, core)

    def slot(axis, step):
        return lax.rem(me[axis] + step + 4, 4)

    sibling = device(x, y, z, 1 - core)
    two = 2 - 4 * lax.rem(z, 2)

    sends = []

    def copy(src, dst, ssem, rsem, to):
        c = pltpu.make_async_remote_copy(
            src_ref=src, dst_ref=dst, send_sem=ssem, recv_sem=rsem, device_id=to, device_id_type=MESH
        )
        c.start()
        sends.append(c)
        return c

    width = D // XCHUNKS
    own = []
    for i in range(XCHUNKS):
        c = pltpu.make_async_copy(
            x_hbm.at[:, pl.ds(i * width, width)], x_own.at[:, pl.ds(i * width, width)], loc_sem.at[i]
        )
        c.start()
        own.append(c)

    bar = pltpu.get_barrier_semaphore()
    greeted = [sibling, peer(2, 4)]
    greeted += [peer(a, d) for a in (0, 1) for d in (1, 2, -1)]
    greeted += [peer(2, d) for d in (1, -1, 2, -2)]
    for to in greeted:
        pl.semaphore_signal(bar, inc=1, device_id=to, device_id_type=MESH)

    mine = w_ref[pl.ds(2 * core, 2)].reshape(HALF, 128)
    gath[me[0], me[1], me[2], pl.ds(core * HALF, HALF), :] = mine.astype(jnp.bfloat16)

    pl.semaphore_wait(bar, len(greeted))

    def ag_view(part, stage, value, low, rows):
        order = AG_ORDER[part]
        idx = [None, None, None]
        for k, axis in enumerate(order):
            idx[axis] = slice(None) if k < stage else (value if k == stage else me[axis])
        return gath.at[idx[0], idx[1], idx[2], pl.ds(core * HALF + PARTS[part][0] + low, rows), :]

    ag = {}

    def ag_send(part, stage):
        axis = AG_ORDER[part][stage]
        rows = PARTS[part][1]
        view = ag_view(part, stage, me[axis], 0, rows)
        ag[part, stage, 0] = copy(view, view, ag_s.at[part, stage, 0], ag_r.at[part, stage, 0], peer(axis, 1))
        ag[part, stage, 1] = copy(view, view, ag_s.at[part, stage, 1], ag_r.at[part, stage, 1], peer(axis, -1))

    def ag_forward(part, stage):
        axis = AG_ORDER[part][stage]
        half = PARTS[part][1] // 2
        ag[part, stage, 0].wait_recv()
        view = ag_view(part, stage, slot(axis, -1), 0, half)
        ag[part, stage, 2] = copy(view, view, ag_s.at[part, stage, 2], ag_r.at[part, stage, 2], peer(axis, 1))
        ag[part, stage, 1].wait_recv()
        view = ag_view(part, stage, slot(axis, 1), half, half)
        ag[part, stage, 3] = copy(view, view, ag_s.at[part, stage, 3], ag_r.at[part, stage, 3], peer(axis, -1))

    def ag_finish(part, stage):
        ag[part, stage, 2].wait_recv()
        ag[part, stage, 3].wait_recv()

    share = {}

    def ag_share(part):
        view = gath.at[:, :, :, pl.ds(core * HALF + PARTS[part][0], PARTS[part][1]), :]
        share[part] = copy(view, view, sh_s.at[part], sh_r.at[part], sibling)

    mv = {}

    def mv_view(n, stage, value):
        axis = MOVE_ORDER[n][stage]
        if stage == 0:
            idx = [slice(None)] * 3
            idx[axis] = value
            return olds[n].at[idx[0], idx[1], idx[2]]
        if stage == 1:
            rest = [a for a in range(3) if a != MOVE_ORDER[n][0]]
            if rest[0] == axis:
                return mids[n].at[0, :, value]
            return mids[n].at[0, :, :, value]
        return mids[n].at[1, :, :, value]

    def mv_send(n, stage):
        axis = MOVE_ORDER[n][stage]
        for k, step in enumerate((1, -1, 2)):
            far = two if (axis == 2 and step == 2) else step
            mv[n, stage, k] = copy(
                mv_view(n, stage, slot(axis, step)), mids[n].at[stage, me[axis]],
                mv_s.at[n, stage, k], mv_r.at[n, stage, k], peer(axis, far),
            )
        mids[n][stage, me[axis]] = mv_view(n, stage, me[axis])[...]

    def mv_finish(n, stage):
        for k in range(3):
            mv[n, stage, k].wait_recv()

    rs = {}

    def rs_view(part, stage, value, low, rows):
        order = RS_ORDER[part]
        idx = [None, None, None]
        for k, axis in enumerate(order):
            idx[axis] = me[axis] if k < stage else (value if k == stage else slice(None))
        return grad.at[idx[0], idx[1], idx[2], pl.ds(PARTS[part][0] + low, rows), :]

    def rs_buf(part, which, stage, low, rows):
        ref = recv[part][which]
        if stage == 0:
            return ref.at[:, pl.ds(0, 4), pl.ds(low, rows), :]
        if stage == 1:
            return ref.at[:, 4, pl.ds(low, rows), :]
        return ref.at[0, 5, pl.ds(low, rows), :]

    def rs_copy(part, stage, k, value, low, rows, which, at, step):
        axis = RS_ORDER[part][stage]
        rs[part, stage, k] = copy(
            rs_view(part, stage, value, low, rows), rs_buf(part, which, stage, at, rows),
            rs_s.at[part, stage, k], rs_r.at[part, stage, k], peer(axis, step),
        )

    def rs_send(part, stage):
        axis = RS_ORDER[part][stage]
        half = PARTS[part][1] // 2
        opposite, right, left = slot(axis, 2), slot(axis, 1), slot(axis, -1)
        rs_copy(part, stage, 0, opposite, 0, half, 2, 0, 1)
        rs_copy(part, stage, 1, opposite, half, half, 3, 0, -1)
        rs_copy(part, stage, 2, right, half, half, 0, half, 1)
        rs_copy(part, stage, 3, left, 0, half, 1, 0, -1)

    def add(view, *others):
        total = view[...].astype(jnp.float32)
        for o in others:
            total = total + o[...].astype(jnp.float32)
        return total.astype(jnp.bfloat16)

    def rs_forward(part, stage):
        axis = RS_ORDER[part][stage]
        half = PARTS[part][1] // 2
        right, left = slot(axis, 1), slot(axis, -1)
        rs[part, stage, 0].wait_recv()
        view = rs_view(part, stage, right, 0, half)
        view[...] = add(view, rs_buf(part, 2, stage, 0, half))
        rs_copy(part, stage, 4, right, 0, half, 0, 0, 1)
        rs[part, stage, 1].wait_recv()
        view = rs_view(part, stage, left, half, half)
        view[...] = add(view, rs_buf(part, 3, stage, 0, half))
        rs_copy(part, stage, 5, left, half, half, 1, half, -1)

    def rs_finish(part, stage):
        axis = RS_ORDER[part][stage]
        rows = PARTS[part][1]
        for k in (2, 3, 4, 5):
            rs[part, stage, k].wait_recv()
        view = rs_view(part, stage, me[axis], 0, rows)
        total = add(view, rs_buf(part, 0, stage, 0, rows), rs_buf(part, 1, stage, 0, rows))
        if stage < 2:
            view[...] = total
        else:
            zsend[pl.ds(PARTS[part][0], rows), :] = total
            rs[part, 3] = copy(
                zsend.at[pl.ds(PARTS[part][0], rows), :], zrecv.at[pl.ds(PARTS[part][0], rows), :],
                fin_s.at[part], fin_r.at[part], peer(2, 4),
            )

    for part in range(3):
        ag_send(part, 0)
    cot_copy = copy(
        cot_ref.at[:, pl.ds(pl.multiple_of((1 - core) * HALF, HALF), HALF)], cot_sib,
        xs_sem.at[XCHUNKS], xr_sem.at[XCHUNKS], sibling,
    )
    xcopy = []
    for i in range(XCHUNKS):
        xcopy.append(
            copy(
                x_hbm.at[:, pl.ds(i * width, width)], x_sib.at[:, pl.ds(i * width, width)],
                xs_sem.at[i], xr_sem.at[i], sibling,
            )
        )
    for n in range(3):
        mv_send(n, 0)
    for part in range(3):
        ag_forward(part, 0)
    cot_copy.wait_recv()
    cot_half = cot_ref[:, pl.ds(pl.multiple_of(core * HALF, HALF), HALF)]
    cot_t[:, pl.ds(0, TOK)] = cot_half.astype(jnp.float32).T.astype(jnp.bfloat16)
    cot_t[:, pl.ds(TOK, TOK)] = cot_sib[...].astype(jnp.float32).T.astype(jnp.bfloat16)
    for part in range(3):
        ag_finish(part, 0)
        ag_send(part, 1)

    def grad_chunk(i):
        at = pl.ds(pl.multiple_of(i * 512, 512), 512)
        total = jnp.dot(cot_t[:, pl.ds(0, TOK)], x_own[:, at], preferred_element_type=jnp.float32)
        total = total + jnp.dot(cot_t[:, pl.ds(TOK, TOK)], x_sib[:, at], preferred_element_type=jnp.float32)
        total = (total * (1.0 / 256.0)).astype(jnp.bfloat16)
        for k in range(4):
            grad[i // 4, lax.rem(i, 4), k] = total[:, k * 128:(k + 1) * 128]

    def grad_span(first, last):
        def body(i, carry):
            grad_chunk(i)
            return carry

        lax.fori_loop(first, last, body, 0)

    for i in range(2):
        own[i].wait()
        xcopy[i].wait_recv()
        grad_span(4 * i, 4 * i + 4)
    for part in range(3):
        ag_forward(part, 1)
    for n in range(3):
        mv_finish(n, 0)
        mv_send(n, 1)
    for i in range(2, 4):
        own[i].wait()
        xcopy[i].wait_recv()
        grad_span(4 * i, 4 * i + 4)
    for part in range(3):
        ag_finish(part, 1)
        ag_send(part, 2)
    for part in range(3):
        rs_send(part, 0)
    for n in range(3):
        mv_finish(n, 1)
        mv_send(n, 2)
    for part in range(3):
        ag_forward(part, 2)
    for part in range(3):
        rs_forward(part, 0)
    for part in range(3):
        ag_finish(part, 2)
        ag_share(part)
    for part in range(3):
        rs_finish(part, 0)
        rs_send(part, 1)
    for part in range(3):
        share[part].wait_recv()

    acc[...] = jnp.zeros_like(acc)

    def block(i):
        p = inv_ref[i]
        return p // 16, lax.rem(p // 4, 4), lax.rem(p, 4)

    def project(t, carry):
        rows = pl.ds(pl.multiple_of(t * 32, 32), 32)
        for k in range(32):
            a = block(2 * k)
            b = block(2 * k + 1)
            first = gath[a[0], a[1], a[2], rows, :].astype(jnp.float32).reshape(4, 8, 128)
            second = gath[b[0], b[1], b[2], rows, :].astype(jnp.float32).reshape(4, 8, 128)
            both = jnp.concatenate([first, second], axis=1).astype(jnp.bfloat16)
            for j in range(4):
                wcol[pl.ds(16 * k, 16), pl.ds(128 * j, 128)] = both[j]
        at = pl.ds(pl.multiple_of(t * 512, 512), 512)
        acc[...] += lax.dot_general(
            x_own[:, at], wcol[...], (((1,), (1,)), ((), ())), preferred_element_type=jnp.float32
        )
        gin_ref[:, at] = jnp.dot(cot_ref[...], wcol[...], preferred_element_type=jnp.float32).astype(
            jnp.bfloat16
        )
        return carry

    lax.fori_loop(0, 8, project, 0)
    for part in range(3):
        rs_forward(part, 1)
    lax.fori_loop(8, 16, project, 0)
    val_ref[...] = acc[...].astype(jnp.bfloat16)
    for part in range(3):
        rs_finish(part, 1)
        rs_send(part, 2)
    for n in range(3):
        mv_finish(n, 2)
    for part in range(3):
        rs_forward(part, 2)
    for part in range(3):
        rs_finish(part, 2)
    for part in range(3):
        rs[part, 3].wait_recv()
    half_rows = pl.ds(pl.multiple_of(core * HALF, HALF), HALF)
    gfull[half_rows, :] = zsend[...].astype(jnp.float32) + zrecv[...].astype(jnp.float32)
    last = copy(gfull.at[half_rows, :], gfull.at[half_rows, :], fin_s.at[3], fin_r.at[3], sibling)
    last.wait_recv()

    def restored(n):
        order = MOVE_ORDER[n]
        rows = []
        for i in range(64):
            p = block(i)
            rows.append(mids[n][2, p[order[2]], p[order[1]], p[order[0]]])
        return jnp.concatenate(rows, axis=0)

    gradient = gfull[...]
    weight = restored(0)
    first_new = beta_one * restored(1) + (1.0 - beta_one) * gradient
    second_new = beta_two * restored(2) + (1.0 - beta_two) * gradient * gradient
    corrected = (
        first_new
        / (1.0 - beta_one**ADAM_STEP)
        / (jnp.sqrt(second_new / (1.0 - beta_two**ADAM_STEP)) + epsilon)
    )
    weight_new = weight - learn_rate * (corrected + decay_rate * weight)
    nw_ref[...] = weight_new.T
    nf_ref[...] = first_new.T
    ns_ref[...] = second_new.T

    for c in sends:
        c.wait_send()


def on_device(inputs, cotangent, old_weight, old_first, old_second, holder):
    slots = jnp.arange(64, dtype=jnp.int32)
    inverse = jnp.sum(jnp.where(holder[None, :] == slots[:, None], slots[None, :], 0), axis=1)

    def tiles(a):
        return a.reshape(8, 64, 128).transpose(1, 0, 2).reshape(4, 4, 4, 8, 128)

    bf, f32 = jnp.bfloat16, jnp.float32
    vmem = pl.BlockSpec(memory_space=pltpu.VMEM)
    dma = pltpu.SemaphoreType.DMA
    buffers = []
    for _, rows in PARTS:
        buffers += [pltpu.VMEM((4, 6, rows, 128), bf)] * 2 + [pltpu.VMEM((4, 6, rows // 2, 128), bf)] * 2
    return pl.pallas_call(
        kernel,
        out_shape=(
            jax.ShapeDtypeStruct((TOK, KV), bf),
            jax.ShapeDtypeStruct((TOK, D), bf),
            jax.ShapeDtypeStruct((128, KV), f32),
            jax.ShapeDtypeStruct((128, KV), f32),
            jax.ShapeDtypeStruct((128, KV), f32),
        ),
        in_specs=[pl.BlockSpec(memory_space=pl.ANY)] + [vmem] * 4 + [pl.BlockSpec(memory_space=pltpu.SMEM)],
        out_specs=(vmem,) * 5,
        scratch_shapes=[
            pltpu.VMEM((TOK, D), bf),
            pltpu.VMEM((TOK, D), bf),
            pltpu.VMEM((TOK, HALF), bf),
            pltpu.VMEM((HALF, 2 * TOK), bf),
            pltpu.VMEM((4, 4, 4, HALF, 128), bf),
            pltpu.VMEM((4, 4, 4, KV, 128), bf),
            pltpu.VMEM((KV, 512), bf),
            pltpu.VMEM((TOK, KV), f32),
            *buffers,
            *[pltpu.VMEM((3, 4, 4, 4, 8, 128), f32)] * 3,
            pltpu.VMEM((HALF, 128), bf),
            pltpu.VMEM((HALF, 128), bf),
            pltpu.VMEM((KV, 128), f32),
            dma((XCHUNKS,)),
            dma((XCHUNKS + 1,)),
            dma((XCHUNKS + 1,)),
            dma((3, 3, 4)),
            dma((3, 3, 4)),
            dma((3,)),
            dma((3,)),
            dma((3, 3, 6)),
            dma((3, 3, 6)),
            dma((3, 3, 3)),
            dma((3, 3, 3)),
            dma((4,)),
            dma((4,)),
        ],
        compiler_params=pltpu.CompilerParams(
            collective_id=0, has_side_effects=True, vmem_limit_bytes=58 * 2**20
        ),
    )(inputs, cotangent, tiles(old_weight), tiles(old_first), tiles(old_second), inverse)


def solution(mesh):
    rows = P(("dp", "fsdp"), None)
    shard = P("fsdp", None)
    return jax.shard_map(
        on_device,
        mesh=mesh,
        in_specs=(rows, rows, shard, shard, shard, P()),
        out_specs=(rows, rows, shard, shard, shard),
        check_vma=False,
    )
```

time: 903 us -> 105 us (0.12)
  waiting for transfers between devices: 805 us -> 0 us
  Pallas kernels: 0 us -> 94.3 us
  matrix products: 25 us -> 0 us
  blocking collectives: 21 us -> 0 us
  starting transfers between devices: 20.4 us -> 0 us
  between operations: 13.9 us -> 0.64 us
    reduce_scatter x1 -> x0, waiting for transfers between devices: 419 us -> none  [on_device(): lax.psum_scatter(lax.dot_general(inputs, cotangent, (((0,), (0,)), ((), (...]
    all_gather x1 -> x0, waiting for transfers between devices: 280 us -> none  [on_device(): lax.all_gather(weight.astype(jnp.bfloat16), 'fsdp', axis=0, tiled=True)]
    pallas_call x0 -> x1, Pallas kernels: none -> 94.3 us  [on_device(): pl.pallas_call(kernel, out_shape=(jax.ShapeDtypeStruct((TOK, KV), bf), ja...]
    psum x1 -> x0, waiting for transfers between devices: 81.1 us -> none  [on_device(): lax.psum(partial_sum.astype(jnp.bfloat16), 'dp').astype(jnp.float32)]
    all_to_all x2 -> x0, waiting for transfers between devices: 25.3 us -> none  [the longest x1 17.1 us: on_device(): lax.all_to_all(old_second, 'fsdp', split_axis=1, concat_axis=0, tiled=True)]
    dot_general x3 -> x0, matrix products: 25 us -> none  [the longest x1 10.3 us: on_device(): lax.dot_general(inputs, cotangent, (((0,), (0,)), ((), ())), preferred_el...]
    all_to_all x1 -> x0, blocking collectives: 21 us -> none  [on_device(): lax.all_to_all(old_first, 'fsdp', split_axis=1, concat_axis=0, tiled=True)]
    all_to_all x2 -> x0, starting transfers between devices: 20.2 us -> none  [the longest x1 12.7 us: on_device(): lax.all_to_all(old_weight, 'fsdp', split_axis=1, concat_axis=0, tiled=True)]
  transfers between devices with their start and end apart: 5 -> 0, of which waited for: 5 -> 0; matrix products, arithmetic and copies ran while one was open for 4% -> 0% of each run, Pallas kernels for 0% -> 0%
where the time goes in v1:
time: 105 us
  Pallas kernels  94.3 us (90%)
  local copies, waits for them, and re-layouts  8.5 us (8%)
  other arithmetic  1.28 us (1%)
    pallas_call x1, Pallas kernels, on_device(): pl.pallas_call(kernel, out_shape=(jax.ShapeDtypeStruct((TOK, KV), bf), ja...  94.3 us
    unnamed x11, local copies, waits for them, and re-layouts  8.5 us

profile of v1, /device:TPU:1, one launch (start us, length us, event | category | flops | bytes accessed | tf_op | source)
XLA Modules:
  0.0 104.7 jit_solution(18401936405101986574)
XLA Ops:
  0.6 1.3 %select_reduce_fusion.inv_ref = s32[64]{0:T(128)} fusion(s32[64]{0:T(128)} %param.11), kind=kLoop, calls=%fused_computation | loop fusion | flops 12224 | bytes 512 | tf_op jit(solution)/shard_map/reduce_sum | solution.py:378
  1.9 94.3 %shard_map.101 = (bf16[256,512]{1,0:T(8,128)(2,1)}, bf16[256,8192]{1,0:T(8,128)(2,1)}, f32[128,512]{1,0:T(8,128)}, f32[128,512]{1,0:T(8,128)}, f32[128,512]{1,0:T(8,128)}) custom-call(bf16[256,8192]{1,0:T(8,128)(2,1)} %x_hbm.1, bf16[256,512]{1,0:T(8,128)(2,1)} %cot_ref.1, f32[4,4,4,8,128]{4,3,2,1,0:T(8,128)} %bitcast.15, f32[4,4,4,8,128]{4,3,2,1,0:T(8,128)} %bitcast.16, ...), custom_call_target="tpu_custom_call" | custom-call | tf_op jit(solution)/shard_map/pallas_call | solution.py:389
  96.2 1.7 %copy.16 = bf16[256,512]{1,0:T(8,128)(2,1)} copy(bf16[256,512]{1,0:T(8,128)(2,1)} %get-tuple-element.10) | data formatting | bytes 524288
  97.9 0.0 copy-start.2
  97.9 0.0 copy-start.1
  97.9 0.0 copy-start
  97.9 4.7 %copy.17 = bf16[256,8192]{1,0:T(8,128)(2,1)} copy(bf16[256,8192]{1,0:T(8,128)(2,1)} %get-tuple-element.11) | data formatting | bytes 8388608
  102.6 0.0 copy-done.2
  102.6 0.7 copy.18
  103.3 0.0 copy-done.1
  103.3 0.7 copy.19
  104.0 0.0 copy-done
  104.0 0.7 copy.20
Async XLA Ops:
  97.9 4.7 %copy-start.2 = (f32[128,512]{1,0:T(8,128)S(1)}, f32[128,512]{1,0:T(8,128)}, u32[]{:S(2)}) copy-start(f32[128,512]{1,0:T(8,128)} %get-tuple-element.12) | copy-start | bytes 786436
  97.9 5.4 %copy-start.1 = (f32[128,512]{1,0:T(8,128)S(1)}, f32[128,512]{1,0:T(8,128)}, u32[]{:S(2)}) copy-start(f32[128,512]{1,0:T(8,128)} %get-tuple-element.13) | copy-start | bytes 786436
  97.9 6.1 %copy-start = (f32[128,512]{1,0:T(8,128)S(1)}, f32[128,512]{1,0:T(8,128)}, u32[]{:S(2)}) copy-start(f32[128,512]{1,0:T(8,128)} %get-tuple-element.14) | copy-start | bytes 786436

commit v2 on v1

v2 whole, which is shorter than its diff:
```python
import functools

import jax
import jax.numpy as jnp
from jax import lax
from jax.experimental import pallas as pl
from jax.experimental.pallas import tpu as pltpu
from jax.sharding import PartitionSpec as P

ADAM_STEP = 20
beta_one = 0.9
beta_two = 0.95
epsilon = 1e-08
decay_rate = 0.1
learn_rate = 0.001

MESH = pl.DeviceIdType.MESH
TOK, D, KV = 256, 8192, 512
HALF = KV // 2
PARTS = ((0, 96), (96, 96), (192, 64))
RS_ORDER = ((0, 1, 2), (1, 2, 0), (2, 0, 1))
AG_ORDER = ((2, 1, 0), (0, 2, 1), (1, 0, 2))
MOVE_ORDER = ((0, 1, 2), (1, 2, 0), (2, 0, 1))
XCHUNKS = 4


def device(x, y, z, core):
    return ((z // 4) * 2 + core, x * 16 + y * 4 + lax.rem(z, 4))


def coordinates():
    dp = lax.axis_index("dp")
    f = lax.axis_index("fsdp")
    core = lax.rem(dp, 2)
    return f // 16, lax.rem(f // 4, 4), (dp // 2) * 4 + lax.rem(f, 4), core


def kernel(
    x_hbm, cot_hbm, w_hbm, f_hbm, s_hbm, holder_ref,
    val_ref, gin_ref, gfull, new_a, new_b, new_c,
    cot_ref, w_ref, f_ref, s_ref, x_own, x_sib, cot_sib, cot_t, grad, gath, pair, order_ref, cot_sur, acc,
    in_0, in_1, in_2, next_0, next_1, next_2, last_in,
    mid_a, mid_b, mid_c, zsend, zrecv,
    loc_sem, pair_s, pair_r, xs_sem, xr_sem, ag_s, ag_r, ag2_s, ag2_r, sh_s, sh_r,
    rs0_s, rs0_r, rs_s, rs_r, mv_s, mv_r, ms_s, ms_r, fin_s, fin_r,
):
    x, y, z, core = coordinates()
    real = (x, y, z)
    size = (4, 4, 8)
    me = (x, y, lax.rem(z, 4))
    olds = (w_ref, f_ref, s_ref)
    mids = (mid_a, mid_b, mid_c)
    news = (new_a, new_b, new_c)
    first_in = (in_0, in_1, in_2)
    second_in = (next_0, next_1, next_2)

    def peer(axis, step):
        at = list(real)
        at[axis] = lax.rem(at[axis] + step + size[axis], size[axis])
        return device(*at, core)

    def slot(axis, step):
        return lax.rem(me[axis] + step + 4, 4)

    sibling = device(x, y, z, 1 - core)
    two = 2 - 4 * lax.rem(z, 2)
    sends = []

    def plan(src, dst, ssem, rsem, to):
        return pltpu.make_async_remote_copy(
            src_ref=src, dst_ref=dst, send_sem=ssem, recv_sem=rsem, device_id=to, device_id_type=MESH
        )

    def copy(src, dst, ssem, rsem, to):
        c = plan(src, dst, ssem, rsem, to)
        c.start()
        sends.append(c)
        return c

    small = []
    for i, (src, dst) in enumerate(((w_hbm, w_ref), (cot_hbm, cot_ref), (f_hbm, f_ref), (s_hbm, s_ref))):
        c = pltpu.make_async_copy(src, dst, loc_sem.at[XCHUNKS + i])
        c.start()
        small.append(c)
    width = D // XCHUNKS
    own = []
    for i in range(XCHUNKS):
        c = pltpu.make_async_copy(
            x_hbm.at[:, pl.ds(i * width, width)], x_own.at[:, pl.ds(i * width, width)], loc_sem.at[i]
        )
        c.start()
        own.append(c)

    bar = pltpu.get_barrier_semaphore()
    greeted = [sibling, peer(2, 4)]
    greeted += [peer(a, d) for a in (0, 1) for d in (1, 2, -1)]
    greeted += [peer(2, d) for d in (1, -1, 2, -2)]
    for to in greeted:
        pl.semaphore_signal(bar, inc=1, device_id=to, device_id_type=MESH)

    small[0].wait()
    pl.semaphore_wait(bar, len(greeted))

    def ag_view(part, at, low, rows):
        if isinstance(at[2], slice):
            pairs, member = at[2], at[2]
        else:
            pairs, member = at[2] // 2, lax.rem(at[2], 2)
        return gath.at[at[0], at[1], pairs, member, pl.ds(core * HALF + PARTS[part][0] + low, rows), :]

    ag = {}

    def ag_send(part, stage):
        order = AG_ORDER[part]
        axis = order[stage]
        rows = PARTS[part][1]
        half = rows // 2
        at = list(me)
        for a in order[:stage]:
            at[a] = slice(None)
        for k, (step, low, n) in enumerate(((1, 0, rows), (-1, 0, rows), (2, 0, half), (-2, half, half))):
            view = ag_view(part, at, low, n)
            ag[part, stage, k] = copy(
                view, view, ag_s.at[part, stage, k], ag_r.at[part, stage, k], peer(axis, step)
            )

    def ag_finish(part, stage):
        for k in range(4):
            ag[part, stage, k].wait_recv()

    def ag2_at(part, value):
        at = [slice(None)] * 3
        at[AG_ORDER[part][2]] = value
        return at

    def ag2_send(part):
        axis = AG_ORDER[part][2]
        view = ag_view(part, ag2_at(part, me[axis]), 0, PARTS[part][1])
        for k, step in enumerate((1, -1)):
            ag[part, 2, k] = copy(view, view, ag2_s.at[part, k], ag2_r.at[part, k], peer(axis, step))

    def ag2_forward(part):
        axis = AG_ORDER[part][2]
        half = PARTS[part][1] // 2
        for k, (step, low) in enumerate(((1, 0), (-1, half))):
            ag[part, 2, k].wait_recv()
            view = ag_view(part, ag2_at(part, slot(axis, -step)), low, half)
            ag[part, 2, 2 + k] = copy(view, view, ag2_s.at[part, 2 + k], ag2_r.at[part, 2 + k], peer(axis, step))

    def ag2_finish(part):
        ag[part, 2, 2].wait_recv()
        ag[part, 2, 3].wait_recv()

    share = {}

    def ag_share(part):
        view = ag_view(part, (slice(None),) * 3, 0, PARTS[part][1])
        share[part] = copy(view, view, sh_s.at[part], sh_r.at[part], sibling)

    mv = {}
    active = [lax.rem(me[MOVE_ORDER[n][2]], 2) == core for n in range(3)]

    def mv_view(n, stage, value):
        axis = MOVE_ORDER[n][stage]
        if stage == 0:
            idx = [slice(None)] * 3
            idx[axis] = value
            return olds[n].at[idx[0], idx[1], idx[2]]
        if stage == 1:
            rest = [a for a in range(3) if a != MOVE_ORDER[n][0]]
            if rest[0] == axis:
                return mids[n].at[0, :, value]
            return mids[n].at[0, :, :, value]
        return mids[n].at[1, :, :, value]

    def mv_dst(n, stage, value):
        return news[n].at[value] if stage == 2 else mids[n].at[stage, value]

    def mv_send(n, stage):
        axis = MOVE_ORDER[n][stage]
        for k, step in enumerate((1, -1, 2)):
            far = two if (axis == 2 and step == 2) else step
            mv[n, stage, k] = plan(
                mv_view(n, stage, slot(axis, step)), mv_dst(n, stage, me[axis]),
                mv_s.at[n, stage, k], mv_r.at[n, stage, k], peer(axis, far),
            )
        home = mv_dst(n, stage, me[axis])
        here = mv_view(n, stage, me[axis])

        @pl.when(active[n])
        def _():
            for k in range(3):
                mv[n, stage, k].start()
            home[...] = here[...]

    def mv_finish(n, stage):
        @pl.when(active[n])
        def _():
            for k in range(3) if stage < 2 else (2,):
                mv[n, stage, k].wait_recv()

        if stage == 2:
            @pl.when(jnp.logical_not(active[n]))
            def _():
                mv[n, stage, 0].wait_recv()
                mv[n, stage, 1].wait_recv()

    def mv_share(n):
        for k in range(2):
            view = news[n].at[core + 2 * k]
            mv[n, 3, k] = copy(view, view, ms_s.at[n, k], ms_r.at[n, k], sibling)

    rs = {}

    def rs_view(part, stage, value, low, rows):
        order = RS_ORDER[part]
        at = [me[0], me[1], me[2]]
        at[order[stage]] = value
        for a in order[stage + 1:]:
            at[a] = slice(None)
        return grad.at[at[0], at[1], at[2], pl.ds(PARTS[part][0] + low, rows), :]

    def rs_buf(part, stage, which, low, rows):
        if stage == 0:
            return first_in[part].at[which, :, :, pl.ds(low, rows), :]
        if stage == 1:
            return second_in[part].at[which, :, pl.ds(low, rows), :]
        return last_in.at[which, pl.ds(PARTS[part][0] + low, rows), :]

    def rs0_copy(part, k, value, low, rows, which, step):
        axis = RS_ORDER[part][0]
        rs[part, 0, k] = copy(
            rs_view(part, 0, value, low, rows), rs_buf(part, 0, which, low, rows),
            rs0_s.at[part, k], rs0_r.at[part, k], peer(axis, step),
        )

    def rs0_far(part):
        axis = RS_ORDER[part][0]
        half = PARTS[part][1] // 2
        rs0_copy(part, 0, slot(axis, 2), 0, half, 2, 1)
        rs0_copy(part, 1, slot(axis, 2), half, half, 2, -1)

    def rs0_near(part):
        axis = RS_ORDER[part][0]
        half = PARTS[part][1] // 2
        rs0_copy(part, 2, slot(axis, 1), half, half, 0, 1)
        rs0_copy(part, 3, slot(axis, -1), 0, half, 1, -1)

    def add(view, *others):
        total = view[...].astype(jnp.float32)
        for o in others:
            total = total + o[...].astype(jnp.float32)
        return total.astype(jnp.bfloat16)

    def rs0_forward(part):
        axis = RS_ORDER[part][0]
        half = PARTS[part][1] // 2
        for k, (step, low) in enumerate(((1, 0), (-1, half))):
            value = slot(axis, step)
            rs[part, 0, k].wait_recv()
            for i in range(4):
                view = rs_view(part, 0, value, low, half).at[i]
                view[...] = add(view, rs_buf(part, 0, 2, low, half).at[i])
            rs0_copy(part, 4 + k, value, low, half, k, step)

    def rs_copy(part, stage, k, value, low, rows, which, step):
        axis = RS_ORDER[part][stage]
        rs[part, stage, k] = copy(
            rs_view(part, stage, value, low, rows), rs_buf(part, stage, which, low, rows),
            rs_s.at[part, stage - 1, k], rs_r.at[part, stage - 1, k], peer(axis, step),
        )

    def rs_send(part, stage):
        axis = RS_ORDER[part][stage]
        rows = PARTS[part][1]
        half = rows // 2
        rs_copy(part, stage, 0, slot(axis, 1), 0, rows, 0, 1)
        rs_copy(part, stage, 1, slot(axis, -1), 0, rows, 1, -1)
        rs_copy(part, stage, 2, slot(axis, 2), 0, half, 2, 2)
        rs_copy(part, stage, 3, slot(axis, 2), half, half, 2, -2)

    def rs0_finish(part):
        axis = RS_ORDER[part][0]
        rows = PARTS[part][1]
        for k in (2, 3, 4, 5):
            rs[part, 0, k].wait_recv()
        for i in range(4):
            view = rs_view(part, 0, me[axis], 0, rows).at[i]
            view[...] = add(view, *[rs_buf(part, 0, which, 0, rows).at[i] for which in range(2)])
        rs_send(part, 1)

    def rs_finish(part, stage):
        rows = PARTS[part][1]
        for k in range(4):
            rs[part, stage, k].wait_recv()
        view = rs_view(part, stage, me[RS_ORDER[part][stage]], 0, rows)
        total = add(view, *[rs_buf(part, stage, which, 0, rows) for which in range(3)])
        if stage == 1:
            view[...] = total
            rs_send(part, 2)
        else:
            lines = pl.ds(PARTS[part][0], rows)
            zsend[lines, :] = total
            rs[part, 3] = copy(
                zsend.at[lines, :], zrecv.at[lines, :], fin_s.at[part], fin_r.at[part], peer(2, 4)
            )

    def grad_chunk(i, carry):
        at = pl.ds(pl.multiple_of(i * 512, 512), 512)
        total = jnp.dot(cot_t[:, pl.ds(0, TOK)], x_own[:, at], preferred_element_type=jnp.float32)
        total = total + jnp.dot(cot_t[:, pl.ds(TOK, TOK)], x_sib[:, at], preferred_element_type=jnp.float32)
        total = (total * (1.0 / 256.0)).astype(jnp.bfloat16)
        for k in range(4):
            grad[i // 4, lax.rem(i, 4), k] = total[:, k * 128:(k + 1) * 128]
        return carry

    def project(t, carry):
        rows = pl.ds(pl.multiple_of((t // 8) * HALF + lax.rem(t, 4) * 64, 64), 64)
        tiles = gath[:, :, :, lax.rem(t // 4, 2), rows, :]
        columns = jnp.concatenate(
            [tiles[:, :, :, 16 * j:16 * j + 16, :].reshape(KV, 128) for j in range(4)], axis=1
        )
        at = pl.ds(pl.multiple_of(t * 512, 512), 512)
        acc[...] += lax.dot_general(
            x_own[:, at], columns, (((1,), (1,)), ((), ())), preferred_element_type=jnp.float32
        )
        gin_ref[:, at] = jnp.dot(cot_sur[...], columns, preferred_element_type=jnp.float32).astype(
            jnp.bfloat16
        )
        return carry

    parity = lax.rem(z, 2)
    pair_copy = copy(
        w_ref.at[2 * core + 1 - parity], pair, pair_s.at[0], pair_r.at[0], peer(2, 1 - 2 * parity)
    )
    for c in small[1:]:
        c.wait()
    cot_copy = copy(
        cot_ref.at[:, pl.ds(pl.multiple_of((1 - core) * HALF, HALF), HALF)], cot_sib,
        xs_sem.at[XCHUNKS], xr_sem.at[XCHUNKS], sibling,
    )
    for n in range(3):
        mv_send(n, 0)
    xcopy = []
    for i in range(XCHUNKS):
        xcopy.append(
            copy(
                x_hbm.at[:, pl.ds(i * width, width)], x_sib.at[:, pl.ds(i * width, width)],
                xs_sem.at[i], xr_sem.at[i], sibling,
            )
        )
    mine = w_ref[2 * core + parity].reshape(16, 8, 128)
    pair_copy.wait_recv()
    other = pair[...].reshape(16, 8, 128)
    both = jnp.concatenate(
        [jnp.where(parity == 0, mine, other), jnp.where(parity == 0, other, mine)], axis=1
    )
    gath[me[0], me[1], me[2] // 2, parity, pl.ds(core * HALF, HALF), :] = both.reshape(HALF, 128).astype(
        jnp.bfloat16
    )
    for part in range(3):
        ag_send(part, 0)
    lane_block = lax.broadcasted_iota(jnp.int32, (1, KV), 1) // 8
    target = lax.rem(lax.broadcasted_iota(jnp.int32, (1, KV), 1), 8)
    for p in range(64):
        target = jnp.where(lane_block == p, target + 8 * holder_ref[p], target)
    hit = lax.broadcasted_iota(jnp.int32, (KV, KV), 0) == target
    order_ref[...] = jnp.where(hit, 1.0, 0.0).astype(jnp.bfloat16)
    cot_sur[...] = jnp.dot(cot_ref[...], order_ref[...], preferred_element_type=jnp.float32).astype(jnp.bfloat16)
    for part in range(3):
        ag_finish(part, 0)
        ag_send(part, 1)
    cot_copy.wait_recv()
    cot_half = cot_ref[:, pl.ds(pl.multiple_of(core * HALF, HALF), HALF)]
    cot_t[:, pl.ds(0, TOK)] = cot_half.astype(jnp.float32).T.astype(jnp.bfloat16)
    cot_t[:, pl.ds(TOK, TOK)] = cot_sib[...].astype(jnp.float32).T.astype(jnp.bfloat16)
    for n in range(3):
        mv_finish(n, 0)
        mv_send(n, 1)
    for part in range(3):
        ag_finish(part, 1)
        ag2_send(part)
    for i in range(XCHUNKS):
        own[i].wait()
        xcopy[i].wait_recv()
        lax.fori_loop(4 * i, 4 * i + 4, grad_chunk, 0)
    for part in range(3):
        rs0_far(part)
    for n in range(3):
        mv_finish(n, 1)
        mv_send(n, 2)
    for part in range(3):
        rs0_near(part)
    for part in range(3):
        ag2_forward(part)
    for part in range(3):
        rs0_forward(part)
    for part in range(3):
        ag2_finish(part)
        ag_share(part)
    acc[...] = jnp.zeros_like(acc)
    for part in range(3):
        share[part].wait_recv()
    lax.fori_loop(0, 8, project, 0)
    for part in range(3):
        rs0_finish(part)
    for n in range(3):
        mv_finish(n, 2)
        mv_share(n)
    lax.fori_loop(8, 16, project, 0)
    for part in range(3):
        rs_finish(part, 1)
    val_ref[...] = lax.dot_general(
        acc[...].astype(jnp.bfloat16), order_ref[...], (((1,), (1,)), ((), ())),
        preferred_element_type=jnp.float32,
    ).astype(jnp.bfloat16)
    for part in range(3):
        rs_finish(part, 2)
    for n in range(3):
        mv[n, 3, 0].wait_recv()
        mv[n, 3, 1].wait_recv()
    for part in range(3):
        rs[part, 3].wait_recv()
    half_rows = pl.ds(pl.multiple_of(core * HALF, HALF), HALF)
    gfull[half_rows, :] = zsend[...].astype(jnp.float32) + zrecv[...].astype(jnp.float32)
    last = copy(gfull.at[half_rows, :], gfull.at[half_rows, :], fin_s.at[3], fin_r.at[3], sibling)
    last.wait_recv()
    for n in range(3):
        @pl.when(active[n])
        def _(n=n):
            for stage in range(3):
                for k in range(3):
                    mv[n, stage, k].wait_send()
    for c in sends:
        c.wait_send()


def update_kernel(
    holder_ref, val_ref, gin_ref, grad_ref, w_ref, f_ref, s_ref, val_out, gin_out, nw_ref, nf_ref, ns_ref, weight_ref, first_ref, second_ref, sem
):
    copies = [
        pltpu.make_async_copy(gin_ref, gin_out, sem.at[0]),
        pltpu.make_async_copy(val_ref, val_out, sem.at[1]),
    ]
    for c in copies:
        c.start()

    targets = (weight_ref, first_ref, second_ref)
    for p in range(64):
        at = (p // 16, (p // 4) % 4, p % 4)
        rows = pl.ds(pl.multiple_of(holder_ref[p] * 8, 8), 8)
        for ref, order, out in zip((w_ref, f_ref, s_ref), MOVE_ORDER, targets):
            out[rows, :] = ref[at[order[2]], at[order[1]], at[order[0]]]
    gradient = grad_ref[...]
    weight = weight_ref[...]
    first_new = beta_one * first_ref[...] + (1.0 - beta_one) * gradient
    second_new = beta_two * second_ref[...] + (1.0 - beta_two) * gradient * gradient
    corrected = (
        first_new
        / (1.0 - beta_one**ADAM_STEP)
        / (jnp.sqrt(second_new / (1.0 - beta_two**ADAM_STEP)) + epsilon)
    )
    nw_ref[...] = (weight - learn_rate * (corrected + decay_rate * weight)).T
    nf_ref[...] = first_new.T
    ns_ref[...] = second_new.T
    for c in copies:
        c.wait()


def on_device(inputs, cotangent, old_weight, old_first, old_second, holder):
    def tiles(a):
        return a.reshape(8, 64, 128).transpose(1, 0, 2).reshape(4, 4, 4, 8, 128)

    bf, f32 = jnp.bfloat16, jnp.float32
    vmem = pl.BlockSpec(memory_space=pltpu.VMEM)
    smem = pl.BlockSpec(memory_space=pltpu.SMEM)
    anywhere = pl.BlockSpec(memory_space=pl.ANY)
    hbm = pl.BlockSpec(memory_space=pltpu.HBM)
    dma = pltpu.SemaphoreType.DMA
    state = (4, 4, 4, 8, 128)
    parts = pl.pallas_call(
        kernel,
        out_shape=(
            pltpu.VMEM((TOK, KV), bf),
            pltpu.VMEM((TOK, D), bf),
            pltpu.VMEM((KV, 128), f32),
            pltpu.VMEM(state, f32),
            pltpu.VMEM(state, f32),
            pltpu.VMEM(state, f32),
        ),
        in_specs=[hbm] * 5 + [smem],
        out_specs=(vmem,) * 6,
        scratch_shapes=[
            pltpu.VMEM((TOK, KV), bf),
            *[pltpu.VMEM(state, f32)] * 3,
            pltpu.VMEM((TOK, D), bf),
            pltpu.VMEM((TOK, D), bf),
            pltpu.VMEM((TOK, HALF), bf),
            pltpu.VMEM((HALF, 2 * TOK), bf),
            pltpu.VMEM((4, 4, 4, HALF, 128), bf),
            pltpu.VMEM((4, 4, 2, 2, KV, 128), bf),
            pltpu.VMEM((4, 4, 8, 128), f32),
            pltpu.VMEM((KV, KV), bf),
            pltpu.VMEM((TOK, KV), bf),
            pltpu.VMEM((TOK, KV), f32),
            *[pltpu.VMEM((3, 4, 4, rows, 128), bf) for _, rows in PARTS],
            *[pltpu.VMEM((3, 4, rows, 128), bf) for _, rows in PARTS],
            pltpu.VMEM((3, HALF, 128), bf),
            *[pltpu.VMEM((2,) + (4, 4, 4, 8, 128), f32)] * 3,
            pltpu.VMEM((HALF, 128), bf),
            pltpu.VMEM((HALF, 128), bf),
            dma((XCHUNKS + 4,)),
            dma((1,)),
            dma((1,)),
            dma((XCHUNKS + 1,)),
            dma((XCHUNKS + 1,)),
            dma((3, 2, 4)),
            dma((3, 2, 4)),
            dma((3, 4)),
            dma((3, 4)),
            dma((3,)),
            dma((3,)),
            dma((3, 6)),
            dma((3, 6)),
            dma((3, 2, 4)),
            dma((3, 2, 4)),
            dma((3, 3, 3)),
            dma((3, 3, 3)),
            dma((3, 2)),
            dma((3, 2)),
            dma((4,)),
            dma((4,)),
        ],
        compiler_params=pltpu.CompilerParams(
            collective_id=0, has_side_effects=True, vmem_limit_bytes=117 * 2**19
        ),
    )(inputs, cotangent, tiles(old_weight), tiles(old_first), tiles(old_second), holder)
    values, grad_input, gradient, weight, first, second = parts
    shard = jax.ShapeDtypeStruct((128, KV), f32)
    return pl.pallas_call(
        update_kernel,
        out_shape=(
            jax.ShapeDtypeStruct((TOK, KV), bf),
            jax.ShapeDtypeStruct((TOK, D), bf),
            shard,
            shard,
            shard,
        ),
        in_specs=[smem] + [vmem] * 6,
        out_specs=(anywhere, anywhere, vmem, vmem, vmem),
        scratch_shapes=[pltpu.VMEM((KV, 128), f32)] * 3 + [dma((2,))],
        compiler_params=pltpu.CompilerParams(vmem_limit_bytes=16 * 2**20),
    )(holder, values, grad_input, gradient, weight, first, second)


def solution(mesh):
    rows = P(("dp", "fsdp"), None)
    shard = P("fsdp", None)
    return jax.shard_map(
        on_device,
        mesh=mesh,
        in_specs=(rows, rows, shard, shard, shard, P()),
        out_specs=(rows, rows, shard, shard, shard),
        check_vma=False,
    )
```

time: 105 us -> 80.7 us (0.77)
  Pallas kernels: 94.3 us -> 79.9 us
  local copies, waits for them, and re-layouts: 8.5 us -> 0.01 us
  other arithmetic: 1.28 us -> 0 us
    pallas_call x1 -> x2, Pallas kernels: 94.3 us -> 79.9 us  [the longest x1 76.3 us: on_device(): pl.pallas_call(kernel, out_shape=(pltpu.VMEM((TOK, KV), bf), pltpu.VMEM((...]
    unnamed x11 -> x2, local copies, waits for them, and re-layouts: 8.5 us -> 0.01 us
    reduce_sum x1 -> x0, other arithmetic: 1.28 us -> none  [on_device(): jnp.sum(jnp.where(holder[None, :] == slots[:, None], slots[None, :], 0),...]
where the time goes in v2:
time: 80.7 us; the launch traced here: 80.6 us
  Pallas kernels  79.9 us (99%)
    pallas_call x1, Pallas kernels, on_device(): pl.pallas_call(kernel, out_shape=(pltpu.VMEM((TOK, KV), bf), pltpu.VMEM((...  76.3 us
    pallas_call x1, Pallas kernels, on_device(): pl.pallas_call(update_kernel, out_shape=(jax.ShapeDtypeStruct((TOK, KV),...  3.61 us

profile of v2, /device:TPU:1, one launch (start us, length us, event | category | flops | bytes accessed | tf_op | source)
XLA Modules:
  0.0 80.6 jit_solution(15132157105201650782)
XLA Ops:
  0.6 0.0 copy-start
  0.6 76.3 %shard_map.101 = (bf16[256,512]{1,0:T(8,128)(2,1)S(1)}, bf16[256,8192]{1,0:T(8,128)(2,1)S(1)}, f32[512,128]{1,0:T(8,128)S(1)}, f32[4,4,4,8,128]{4,3,2,1,0:T(8,12...) custom-call(bf16[256,8192]{1,0:T(8,128)(2,1)} %x_hbm.1, bf16[256,512]{1,0:T(8,128)(2,1)} %cot_hbm.1, ...), custom_call_target="tpu_custom_call" | custom-call | tf_op jit(solution)/shard_map/pallas_call | solution.py:481
  77.0 0.0 copy-done
  77.0 3.6 %shard_map.102 = (bf16[256,512]{1,0:T(8,128)(2,1)}, bf16[256,8192]{1,0:T(8,128)(2,1)}, f32[128,512]{1,0:T(8,128)}, f32[128,512]{1,0:T(8,128)}, f32[128,512]{1,0:T(8,128)}) custom-call(s32[64]{0:T(128)S(1)} %copy-done, bf16[256,512]{1,0:T(8,128)(2,1)S(1)} %get-tuple-element.11.val_ref, bf16[256,8192]{1,0:T(8,128)(2,1)S(1)} %get-tuple-element.12.gin_ref, ...), custom_call_target="tpu_custom_call" | custom-call | tf_op jit(solution)/shard_map/pallas_call | solution.py:540
Async XLA Ops:
  0.6 76.3 %copy-start = (s32[64]{0:T(128)S(1)}, s32[64]{0:T(128)}, u32[]{:S(2)}) copy-start(s32[64]{0:T(128)} %holder_ref.3) | copy-start | bytes 772

commit v3 on v2

--- a/solution.py
+++ b/solution.py
@@ -84,10 +84,10 @@
         small.append(c)
     width = D // XCHUNKS
     own = []
+    spans = [lax.rem(x + step, 4) for step in (2, 1, 3, 0)]
+    columns_of = [pl.ds(pl.multiple_of(span * width, width), width) for span in spans]
     for i in range(XCHUNKS):
-        c = pltpu.make_async_copy(
-            x_hbm.at[:, pl.ds(i * width, width)], x_own.at[:, pl.ds(i * width, width)], loc_sem.at[i]
-        )
+        c = pltpu.make_async_copy(x_hbm.at[:, columns_of[i]], x_own.at[:, columns_of[i]], loc_sem.at[i])
         c.start()
         own.append(c)
 
@@ -135,9 +135,13 @@
 
     def ag2_send(part):
         axis = AG_ORDER[part][2]
-        view = ag_view(part, ag2_at(part, me[axis]), 0, PARTS[part][1])
-        for k, step in enumerate((1, -1)):
-            ag[part, 2, k] = copy(view, view, ag2_s.at[part, k], ag2_r.at[part, k], peer(axis, step))
+        half = PARTS[part][1] // 2
+        for first in (True, False):
+            for k, step in enumerate((1, -1)):
+                low = 0 if (k == 0) == first else half
+                j = k if first else 4 + k
+                view = ag_view(part, ag2_at(part, me[axis]), low, half)
+                ag[part, 2, j] = copy(view, view, ag2_s.at[part, j], ag2_r.at[part, j], peer(axis, step))
 
     def ag2_forward(part):
         axis = AG_ORDER[part][2]
@@ -148,8 +152,8 @@
             ag[part, 2, 2 + k] = copy(view, view, ag2_s.at[part, 2 + k], ag2_r.at[part, 2 + k], peer(axis, step))
 
     def ag2_finish(part):
-        ag[part, 2, 2].wait_recv()
-        ag[part, 2, 3].wait_recv()
+        for k in (2, 3, 4, 5):
+            ag[part, 2, k].wait_recv()
 
     share = {}
 
@@ -345,7 +349,7 @@
     for i in range(XCHUNKS):
         xcopy.append(
             copy(
-                x_hbm.at[:, pl.ds(i * width, width)], x_sib.at[:, pl.ds(i * width, width)],
+                x_hbm.at[:, columns_of[i]], x_sib.at[:, columns_of[i]],
                 xs_sem.at[i], xr_sem.at[i], sibling,
             )
         )
@@ -360,6 +364,36 @@
     )
     for part in range(3):
         ag_send(part, 0)
+
+    def grad_span(i):
+        own[i].wait()
+        xcopy[i].wait_recv()
+        lax.fori_loop(4 * spans[i], 4 * spans[i] + 4, grad_chunk, 0)
+
+    cot_copy.wait_recv()
+    cot_half = cot_ref[:, pl.ds(pl.multiple_of(core * HALF, HALF), HALF)]
+    cot_t[:, pl.ds(0, TOK)] = cot_half.astype(jnp.float32).T.astype(jnp.bfloat16)
+    cot_t[:, pl.ds(TOK, TOK)] = cot_sib[...].astype(jnp.float32).T.astype(jnp.bfloat16)
+    grad_span(0)
+    rs0_far(0)
+    for part in range(3):
+        ag_finish(part, 0)
+        ag_send(part, 1)
+    grad_span(1)
+    grad_span(2)
+    rs0_near(0)
+    grad_span(3)
+    for part in (1, 2):
+        rs0_far(part)
+    for part in (1, 2):
+        rs0_near(part)
+    for n in range(3):
+        mv_finish(n, 0)
+        mv_send(n, 1)
+    for part in range(3):
+        ag_finish(part, 1)
+        ag2_send(part)
+    rs0_forward(0)
     lane_block = lax.broadcasted_iota(jnp.int32, (1, KV), 1) // 8
     target = lax.rem(lax.broadcasted_iota(jnp.int32, (1, KV), 1), 8)
     for p in range(64):
@@ -367,55 +401,34 @@
     hit = lax.broadcasted_iota(jnp.int32, (KV, KV), 0) == target
     order_ref[...] = jnp.where(hit, 1.0, 0.0).astype(jnp.bfloat16)
     cot_sur[...] = jnp.dot(cot_ref[...], order_ref[...], preferred_element_type=jnp.float32).astype(jnp.bfloat16)
-    for part in range(3):
-        ag_finish(part, 0)
-        ag_send(part, 1)
-    cot_copy.wait_recv()
-    cot_half = cot_ref[:, pl.ds(pl.multiple_of(core * HALF, HALF), HALF)]
-    cot_t[:, pl.ds(0, TOK)] = cot_half.astype(jnp.float32).T.astype(jnp.bfloat16)
-    cot_t[:, pl.ds(TOK, TOK)] = cot_sib[...].astype(jnp.float32).T.astype(jnp.bfloat16)
-    for n in range(3):
-        mv_finish(n, 0)
-        mv_send(n, 1)
-    for part in range(3):
-        ag_finish(part, 1)
-        ag2_send(part)
-    for i in range(XCHUNKS):
-        own[i].wait()
-        xcopy[i].wait_recv()
-        lax.fori_loop(4 * i, 4 * i + 4, grad_chunk, 0)
-    for part in range(3):
-        rs0_far(part)
+    acc[...] = jnp.zeros_like(acc)
+    for part in (1, 2):
+        rs0_forward(part)
     for n in range(3):
         mv_finish(n, 1)
         mv_send(n, 2)
     for part in range(3):
-        rs0_near(part)
-    for part in range(3):
         ag2_forward(part)
     for part in range(3):
-        rs0_forward(part)
+        rs0_finish(part)
     for part in range(3):
         ag2_finish(part)
         ag_share(part)
-    acc[...] = jnp.zeros_like(acc)
-    for part in range(3):
-        share[part].wait_recv()
-    lax.fori_loop(0, 8, project, 0)
-    for part in range(3):
-        rs0_finish(part)
     for n in range(3):
         mv_finish(n, 2)
         mv_share(n)
+    for part in range(3):
+        rs_finish(part, 1)
+    for part in range(3):
+        share[part].wait_recv()
+    lax.fori_loop(0, 8, project, 0)
+    for part in range(3):
+        rs_finish(part, 2)
     lax.fori_loop(8, 16, project, 0)
-    for part in range(3):
-        rs_finish(part, 1)
     val_ref[...] = lax.dot_general(
         acc[...].astype(jnp.bfloat16), order_ref[...], (((1,), (1,)), ((), ())),
         preferred_element_type=jnp.float32,
     ).astype(jnp.bfloat16)
-    for part in range(3):
-        rs_finish(part, 2)
     for n in range(3):
         mv[n, 3, 0].wait_recv()
         mv[n, 3, 1].wait_recv()
@@ -516,8 +529,8 @@
             dma((XCHUNKS + 1,)),
             dma((3, 2, 4)),
             dma((3, 2, 4)),
-            dma((3, 4)),
-            dma((3, 4)),
+            dma((3, 6)),
+            dma((3, 6)),
             dma((3,)),
             dma((3,)),
             dma((3, 6)),

time: 80.7 us -> 75.6 us (0.937)
  Pallas kernels: 79.9 us -> 74.9 us
    pallas_call x1, Pallas kernels: 76.3 us -> 71.3 us  [on_device(): pl.pallas_call(kernel, out_shape=(pltpu.VMEM((TOK, KV), bf), pltpu.VMEM((...]
where the time goes in v3:
time: 75.6 us; the launch traced here: 75.5 us
  Pallas kernels  74.9 us (99%)
    pallas_call x1, Pallas kernels, on_device(): pl.pallas_call(kernel, out_shape=(pltpu.VMEM((TOK, KV), bf), pltpu.VMEM((...  71.3 us
    pallas_call x1, Pallas kernels, on_device(): pl.pallas_call(update_kernel, out_shape=(jax.ShapeDtypeStruct((TOK, KV),...  3.61 us

profile of v3, /device:TPU:1, one launch (start us, length us, event | category | flops | bytes accessed | tf_op | source)
XLA Modules:
  0.0 75.5 jit_solution(3106232373592359384)
XLA Ops:
  0.6 0.0 copy-start
  0.6 71.3 %shard_map.101 = (bf16[256,512]{1,0:T(8,128)(2,1)S(1)}, bf16[256,8192]{1,0:T(8,128)(2,1)S(1)}, f32[512,128]{1,0:T(8,128)S(1)}, f32[4,4,4,8,128]{4,3,2,1,0:T(8,12...) custom-call(bf16[256,8192]{1,0:T(8,128)(2,1)} %x_hbm.1, bf16[256,512]{1,0:T(8,128)(2,1)} %cot_hbm.1, ...), custom_call_target="tpu_custom_call" | custom-call | tf_op jit(solution)/shard_map/pallas_call | solution.py:494
  71.9 0.0 copy-done
  71.9 3.6 %shard_map.102 = (bf16[256,512]{1,0:T(8,128)(2,1)}, bf16[256,8192]{1,0:T(8,128)(2,1)}, f32[128,512]{1,0:T(8,128)}, f32[128,512]{1,0:T(8,128)}, f32[128,512]{1,0:T(8,128)}) custom-call(s32[64]{0:T(128)S(1)} %copy-done, bf16[256,512]{1,0:T(8,128)(2,1)S(1)} %get-tuple-element.11.val_ref, bf16[256,8192]{1,0:T(8,128)(2,1)S(1)} %get-tuple-element.12.gin_ref, ...), custom_call_target="tpu_custom_call" | custom-call | tf_op jit(solution)/shard_map/pallas_call | solution.py:553
Async XLA Ops:
  0.6 71.3 %copy-start = (s32[64]{0:T(128)S(1)}, s32[64]{0:T(128)}, u32[]{:S(2)}) copy-start(s32[64]{0:T(128)} %holder_ref.3) | copy-start | bytes 772

commit v4 on v3

--- a/solution.py
+++ b/solution.py
@@ -387,9 +387,6 @@
         rs0_far(part)
     for part in (1, 2):
         rs0_near(part)
-    for n in range(3):
-        mv_finish(n, 0)
-        mv_send(n, 1)
     for part in range(3):
         ag_finish(part, 1)
         ag2_send(part)
@@ -404,27 +401,30 @@
     acc[...] = jnp.zeros_like(acc)
     for part in (1, 2):
         rs0_forward(part)
+    for part in range(3):
+        ag2_forward(part)
+    for part in range(3):
+        rs0_finish(part)
+    for n in range(3):
+        mv_finish(n, 0)
+        mv_send(n, 1)
+    for part in range(3):
+        ag2_finish(part)
+        ag_share(part)
+    for part in range(3):
+        rs_finish(part, 1)
+    for part in range(3):
+        share[part].wait_recv()
     for n in range(3):
         mv_finish(n, 1)
         mv_send(n, 2)
-    for part in range(3):
-        ag2_forward(part)
-    for part in range(3):
-        rs0_finish(part)
-    for part in range(3):
-        ag2_finish(part)
-        ag_share(part)
+    lax.fori_loop(0, 8, project, 0)
+    for part in range(3):
+        rs_finish(part, 2)
+    lax.fori_loop(8, 16, project, 0)
     for n in range(3):
         mv_finish(n, 2)
         mv_share(n)
-    for part in range(3):
-        rs_finish(part, 1)
-    for part in range(3):
-        share[part].wait_recv()
-    lax.fori_loop(0, 8, project, 0)
-    for part in range(3):
-        rs_finish(part, 2)
-    lax.fori_loop(8, 16, project, 0)
     val_ref[...] = lax.dot_general(
         acc[...].astype(jnp.bfloat16), order_ref[...], (((1,), (1,)), ((), ())),
         preferred_element_type=jnp.float32,
@@ -449,7 +449,8 @@
 
 
 def update_kernel(
-    holder_ref, val_ref, gin_ref, grad_ref, w_ref, f_ref, s_ref, val_out, gin_out, nw_ref, nf_ref, ns_ref, weight_ref, first_ref, second_ref, sem
+    holder_ref, val_ref, gin_ref, grad_ref, w_ref, f_ref, s_ref, val_out, gin_out, nw_ref, nf_ref, ns_ref, weight_ref, first_ref, second_ref,
+    nw_out, nf_out, ns_out, sem
 ):
     copies = [
         pltpu.make_async_copy(gin_ref, gin_out, sem.at[0]),
@@ -464,18 +465,24 @@
         rows = pl.ds(pl.multiple_of(holder_ref[p] * 8, 8), 8)
         for ref, order, out in zip((w_ref, f_ref, s_ref), MOVE_ORDER, targets):
             out[rows, :] = ref[at[order[2]], at[order[1]], at[order[0]]]
+    def leave(i, value, staged, out):
+        staged[...] = value.T
+        c = pltpu.make_async_copy(staged, out, sem.at[i])
+        c.start()
+        copies.append(c)
+
     gradient = grad_ref[...]
+    first_new = beta_one * first_ref[...] + (1.0 - beta_one) * gradient
+    leave(2, first_new, nf_out, nf_ref)
+    second_new = beta_two * second_ref[...] + (1.0 - beta_two) * gradient * gradient
+    leave(3, second_new, ns_out, ns_ref)
     weight = weight_ref[...]
-    first_new = beta_one * first_ref[...] + (1.0 - beta_one) * gradient
-    second_new = beta_two * second_ref[...] + (1.0 - beta_two) * gradient * gradient
     corrected = (
         first_new
         / (1.0 - beta_one**ADAM_STEP)
         / (jnp.sqrt(second_new / (1.0 - beta_two**ADAM_STEP)) + epsilon)
     )
-    nw_ref[...] = (weight - learn_rate * (corrected + decay_rate * weight)).T
-    nf_ref[...] = first_new.T
-    ns_ref[...] = second_new.T
+    leave(4, weight - learn_rate * (corrected + decay_rate * weight), nw_out, nw_ref)
     for c in copies:
         c.wait()
 
@@ -560,8 +567,8 @@
             shard,
         ),
         in_specs=[smem] + [vmem] * 6,
-        out_specs=(anywhere, anywhere, vmem, vmem, vmem),
-        scratch_shapes=[pltpu.VMEM((KV, 128), f32)] * 3 + [dma((2,))],
+        out_specs=(anywhere,) * 5,
+        scratch_shapes=[pltpu.VMEM((KV, 128), f32)] * 3 + [pltpu.VMEM((128, KV), f32)] * 3 + [dma((5,))],
         compiler_params=pltpu.CompilerParams(vmem_limit_bytes=16 * 2**20),
     )(holder, values, grad_input, gradient, weight, first, second)
 

time: 75.6 us -> 73 us (0.966)
  Pallas kernels: 74.9 us -> 72.2 us
    pallas_call x1, Pallas kernels: 71.3 us -> 69.1 us  [on_device(): pl.pallas_call(kernel, out_shape=(pltpu.VMEM((TOK, KV), bf), pltpu.VMEM((...]
where the time goes in v4:
time: 73 us; the launch traced here: 72.9 us
  Pallas kernels  72.2 us (99%)
    pallas_call x1, Pallas kernels, on_device(): pl.pallas_call(kernel, out_shape=(pltpu.VMEM((TOK, KV), bf), pltpu.VMEM((...  69.1 us
    pallas_call x1, Pallas kernels, on_device(): pl.pallas_call(update_kernel, out_shape=(jax.ShapeDtypeStruct((TOK, KV),...  3.1 us

profile of v4, /device:TPU:1, one launch (start us, length us, event | category | flops | bytes accessed | tf_op | source)
XLA Modules:
  0.0 72.9 jit_solution(17819011918684546362)
XLA Ops:
  0.6 0.0 copy-start
  0.6 69.1 %shard_map.101 = (bf16[256,512]{1,0:T(8,128)(2,1)S(1)}, bf16[256,8192]{1,0:T(8,128)(2,1)S(1)}, f32[512,128]{1,0:T(8,128)S(1)}, f32[4,4,4,8,128]{4,3,2,1,0:T(8,12...) custom-call(bf16[256,8192]{1,0:T(8,128)(2,1)} %x_hbm.1, bf16[256,512]{1,0:T(8,128)(2,1)} %cot_hbm.1, ...), custom_call_target="tpu_custom_call" | custom-call | tf_op jit(solution)/shard_map/pallas_call | solution.py:501
  69.8 0.0 copy-done
  69.8 3.1 %shard_map.102 = (bf16[256,512]{1,0:T(8,128)(2,1)}, bf16[256,8192]{1,0:T(8,128)(2,1)}, f32[128,512]{1,0:T(8,128)}, f32[128,512]{1,0:T(8,128)}, f32[128,512]{1,0:T(8,128)}) custom-call(s32[64]{0:T(128)S(1)} %copy-done, bf16[256,512]{1,0:T(8,128)(2,1)S(1)} %get-tuple-element.11.val_ref, bf16[256,8192]{1,0:T(8,128)(2,1)S(1)} %get-tuple-element.12.gin_ref, ...), custom_call_target="tpu_custom_call" | custom-call | tf_op jit(solution)/shard_map/pallas_call | solution.py:560
Async XLA Ops:
  0.6 69.1 %copy-start = (s32[64]{0:T(128)S(1)}, s32[64]{0:T(128)}, u32[]{:S(2)}) copy-start(s32[64]{0:T(128)} %holder_ref.3) | copy-start | bytes 772
